TPU v7x, 32 devices: a whole 2x2x4 slice. The times are simulated.
32 devices in a mesh: seq: 8 (over y, x, core), blk: 4 (over z).
Axes of the slice: x: 2, y: 2, z: 4, core: 2. Of those that a mesh axis runs over, the one named last changes fastest.
Arguments:
- alphas: float32 [2, 512, 32768], P(None, 'seq', 'blk'), may hold values from 0.05 to 1
- betas: float32 [2, 512, 65536], P(None, 'seq', 'blk'), may hold values from 0.05 to 1
- token_ids: int32 [2, 512], P(None, 'seq'), may hold values from 0 to 31
- emission: float32 [32, 65536], P(None, 'blk'), may hold values from 0.05 to 1
- left_blocks: float32 [64, 128, 512], P('blk'), may hold values from 0.000390625 to 0.00390625
- right_blocks: float32 [128, 64, 512], P('blk', 'seq'), may hold values from 0.003125 to 0.03125
Outputs:
- left_grad: float32 [64, 128, 512], P('blk', 'seq')
- right_grad: float32 [128, 64, 512], P('blk', 'seq')
All inputs are finite; a program needn't handle non-finite values.
Results may differ from a plain program's by a relative error of at most 0.0001.
Values sent between devices are 32-bit elements; how exact they have to be, the bound alone decides.
A program may use at most 128 MiB of HBM per device.

v0:
```python
import functools
import jax
import jax.numpy as jnp
from jax import lax
from jax.experimental import pallas as pl
from jax.experimental.pallas import tpu as pltpu
from jax.sharding import PartitionSpec as P

F32 = jnp.float32
BF16 = jnp.bfloat16
CHIPS = 4
CHUNKS = 4


def halves(x):
    top = x.astype(BF16)
    rest = (x - top.astype(F32)).astype(BF16)
    return jnp.concatenate([top, rest], axis=0)


def nt(a, b):
    return lax.dot_general(a, b, (((1,), (1,)), ((), ())), preferred_element_type=F32)


def kernel(
    nz, scale, a_hbm, b_hbm, hot_ref, e_hbm, l_hbm, r_hbm, left_out, right_out,
    a32, b32, e32, l32, a16, g16, rf, us, ur, hs, hr, pr, pl_, rx0r, rx0l, rx1r, rx1l, cs, cr,
    load_a, load_l, load_b, load_e, load_r, own_u, own_h,
    ag_s, ag_r, fw_s, fw_r, u_s, u_r, h_s, h_r, c_s, c_r, s0_s, s0_r, s1_s, s1_r,
):
    seq = lax.axis_index("seq")
    z = lax.axis_index("blk")
    core, chip = seq % 2, seq // 2
    x, y = chip % 2, chip // 2
    sibling = 2 * chip + 1 - core
    chips = (2 * y + 1 - x, 2 * (1 - y) + x, 2 * (1 - y) + 1 - x)
    peers = tuple(2 * other + core for other in chips)
    blocks_here, window, width = l32.shape
    local_k, nblocks = g16.shape[0], g16.shape[2]
    count = a16.shape[1] // 2
    seq_dev = count // 2
    inputs = nz * blocks_here
    part_i, part_k = blocks_here // CHUNKS, local_k // CHUNKS
    rows_z = blocks_here * local_k
    rows_c = part_i * local_k

    loads_a, loads_l, loads_b, loads_e = [], [], [], []
    for n in range(CHUNKS):
        cols = pl.ds(n * part_i * width, part_i * width)
        loads_a.append(pltpu.make_async_copy(a_hbm.at[:, :, cols], a32.at[:, :, cols], load_a.at[n]))
        some = pl.ds(n * part_i, part_i)
        loads_l.append(pltpu.make_async_copy(l_hbm.at[some], l32.at[some], load_l.at[n]))
        cols = pl.ds(n * part_k * nblocks, part_k * nblocks)
        loads_b.append(pltpu.make_async_copy(b_hbm.at[:, :, cols], b32.at[:, :, cols], load_b.at[n]))
        loads_e.append(pltpu.make_async_copy(e_hbm.at[:, cols], e32.at[:, cols], load_e.at[n]))
    load_own = pltpu.make_async_copy(r_hbm, rf.at[seq], load_r)
    load_own.start()
    for n in range(CHUNKS):
        loads_l[n].start()
        loads_a[n].start()
    for n in range(CHUNKS):
        loads_e[n].start()
        loads_b[n].start()

    barrier = pltpu.get_barrier_semaphore()
    for other in (sibling,) + peers:
        pl.semaphore_signal(barrier, inc=1, device_id={"seq": other}, device_id_type=pl.DeviceIdType.MESH)
    for d in range(1, nz):
        pl.semaphore_signal(barrier, inc=1, device_id={"blk": (z + d) % nz}, device_id_type=pl.DeviceIdType.MESH)
    pl.semaphore_wait(barrier, 4 + nz - 1)

    def to_seq(src, dst, send, recv, other):
        return pltpu.make_async_remote_copy(
            src_ref=src, dst_ref=dst, send_sem=send, recv_sem=recv,
            device_id={"seq": other}, device_id_type=pl.DeviceIdType.MESH,
        )

    def to_blk(src, dst, send, recv, other):
        return pltpu.make_async_remote_copy(
            src_ref=src, dst_ref=dst, send_sem=send, recv_sem=recv,
            device_id={"blk": other}, device_id_type=pl.DeviceIdType.MESH,
        )

    gathers = [to_seq(r_hbm, rf.at[seq], ag_s.at[n], ag_r.at[n], other) for n, other in enumerate(peers + (sibling,))]
    for copy in gathers:
        copy.start()

    def u_block(i, _):
        cols = pl.ds(pl.multiple_of(i * width, width), width)
        a = halves(jnp.concatenate([a32[0, :, cols], a32[1, :, cols]], axis=0))
        a16[i] = a
        both = nt(halves(l32[i]), a)
        u = both[:window, :count] + both[:window, count:] + both[window:, :count]
        for dz in range(nz):
            us[pl.ds(dz * rows_z + i * local_k, local_k), :] = u[dz * local_k:(dz + 1) * local_k]
        return 0

    for n in range(CHUNKS):
        loads_l[n].wait()
        loads_a[n].wait()
        lax.fori_loop(n * part_i, (n + 1) * part_i, u_block, 0)
    u_own = pltpu.make_async_copy(us.at[pl.ds(z * rows_z, rows_z)], ur.at[pl.ds(z * rows_z, rows_z)], own_u)
    u_own.start()
    u_sends = []
    for d in range(1, nz):
        other = (z + d) % nz
        copy = to_blk(
            us.at[pl.ds(other * rows_z, rows_z)], ur.at[pl.ds(z * rows_z, rows_z)], u_s.at[d - 1], u_r.at[d - 1], other
        )
        copy.start()
        u_sends.append(copy)

    hot = hot_ref[...]

    def g_block(k, _):
        cols = pl.ds(pl.multiple_of(k * nblocks, nblocks), nblocks)
        e = e32[:, cols]
        e1 = e.astype(BF16)
        rest = e - e1.astype(F32)
        e2 = rest.astype(BF16)
        e3 = (rest - e2.astype(F32)).astype(BF16)
        picked = jnp.dot(hot, jnp.concatenate([e1, e2, e3], axis=0), preferred_element_type=F32)
        b = jnp.concatenate([b32[0, :, cols], b32[1, :, cols]], axis=0)
        g16[k] = halves(picked * b)
        return 0

    for n in range(CHUNKS):
        loads_e[n].wait()
        loads_b[n].wait()
        lax.fori_loop(n * part_k, (n + 1) * part_k, g_block, 0)

    load_own.wait()
    forwards = []
    for n, other in enumerate(peers):
        gathers[n].wait_recv()
        slot = rf.at[other]
        copy = to_seq(slot, slot, fw_s.at[n], fw_r.at[n], sibling)
        copy.start()
        forwards.append(copy)
    gathers[3].wait_recv()
    for copy in forwards:
        copy.wait_recv()

    def h_block(k, _):
        r = halves(jnp.concatenate([rf[s, k] for s in range(2 * CHIPS)], axis=0))
        both = nt(r, g16[k])
        h = both[:inputs, :count] + both[:inputs, count:] + both[inputs:, :count]
        hs[pl.ds(k, inputs, stride=local_k), :] = h
        return 0

    lax.fori_loop(0, local_k, h_block, 0)

    u_own.wait()
    for copy in u_sends:
        copy.wait_recv()
    step = 64

    def c_block(n, acc):
        rows = pl.ds(pl.multiple_of(n * step, step), step)
        return acc + jnp.sum((ur[rows, :] * hs[rows, :]).reshape(step // 8, 8, count), axis=0)

    acc = lax.fori_loop(0, nz * rows_z // step, c_block, jnp.zeros((8, count), F32))
    cs[...] = acc
    c_sends = []
    for d in range(1, nz):
        copy = to_blk(cs, cr.at[d - 1], c_s.at[d - 1], c_r.at[d - 1], (z + d) % nz)
        copy.start()
        c_sends.append(copy)
    h_own = pltpu.make_async_copy(hs.at[pl.ds(z * rows_z, rows_z)], hr.at[pl.ds(z * rows_z, rows_z)], own_h)
    h_own.start()
    h_sends = []
    for n in range(CHUNKS):
        for d in range(1, nz):
            other = (z + d) % nz
            copy = to_blk(
                hs.at[pl.ds(other * rows_z + n * rows_c, rows_c)],
                hr.at[pl.ds(z * rows_z + n * rows_c, rows_c)],
                h_s.at[n, d - 1], h_r.at[n, d - 1], other,
            )
            copy.start()
            h_sends.append(copy)
    total = acc
    for n, copy in enumerate(c_sends):
        copy.wait_recv()
        total = total + cr[n]
    weight = scale / jnp.sum(total, axis=0, keepdims=True)

    def right_part(n):
        def block(kk, _):
            k = n * part_k + kk
            u = halves(ur[pl.ds(k, inputs, stride=local_k), :] * weight)
            both = jnp.dot(jnp.concatenate([u, u], axis=1), g16[k], preferred_element_type=F32)
            grad = both[:inputs] + both[inputs:]
            rows = inputs // (2 * CHIPS)
            for s in range(2 * CHIPS):
                pr[n, s % 2, s // 2, kk] = grad[s * rows:(s + 1) * rows]
            return 0

        lax.fori_loop(0, part_k, block, 0)

    def left_part(n):
        def block(ii, _):
            i = n * part_i + ii
            h = jnp.concatenate(
                [hr[pl.ds(pl.multiple_of(sz * rows_z + i * local_k, local_k), local_k), :] for sz in range(nz)], axis=0
            )
            h = halves(h * weight)
            both = jnp.dot(jnp.concatenate([h, h], axis=1), a16[i], preferred_element_type=F32)
            grad = both[:window] + both[window:]
            rows = window // (2 * CHIPS)
            for s in range(2 * CHIPS):
                pl_[n, s % 2, s // 2, ii] = grad[s * rows:(s + 1) * rows]
            return 0

        lax.fori_loop(0, part_i, block, 0)

    firsts, seconds = {}, {}

    def first(m, mine, into, n):
        firsts[m] = to_seq(mine.at[n, 1 - core], into.at[n], s0_s.at[m], s0_r.at[m], sibling)
        firsts[m].start()

    def second(m, mine, got, into, n):
        firsts[m].wait_recv()

        def add(p, _):
            mine[n, core, p] = mine[n, core, p] + got[n, p]
            return 0

        lax.fori_loop(0, CHIPS, add, 0)
        seconds[m] = []
        for d, other in enumerate(chips):
            copy = to_seq(mine.at[n, core, other], into.at[d, n], s1_s.at[m, d], s1_r.at[m, d], peers[d])
            copy.start()
            seconds[m].append(copy)

    def last(m, mine, into, out, n, part):
        for copy in seconds[m]:
            copy.wait_recv()
        out[n * part:(n + 1) * part] = mine[n, core, chip] + into[0, n] + into[1, n] + into[2, n]

    for m in range(2 * CHUNKS):
        n = m % CHUNKS
        if m < CHUNKS:
            right_part(n)
            first(m, pr, rx0r, n)
        else:
            if n == 0:
                h_own.wait()
            for copy in h_sends[n * (nz - 1):(n + 1) * (nz - 1)]:
                copy.wait_recv()
            left_part(n)
            first(m, pl_, rx0l, n)
        if 1 <= m <= CHUNKS:
            second(m - 1, pr, rx0r, rx1r, m - 1)
        elif m > CHUNKS:
            second(m - 1, pl_, rx0l, rx1l, n - 1)
    second(2 * CHUNKS - 1, pl_, rx0l, rx1l, CHUNKS - 1)
    for n in range(CHUNKS):
        last(n, pr, rx1r, right_out, n, part_k)
    for n in range(CHUNKS):
        last(CHUNKS + n, pl_, rx1l, left_out, n, part_i)

    for copy in gathers + forwards + u_sends + c_sends + h_sends + list(firsts.values()):
        copy.wait_send()
    for copies in seconds.values():
        for copy in copies:
            copy.wait_send()


def fused(alphas, betas, token_ids, emission, left_blocks, right_blocks):
    nz = lax.axis_size("blk")
    seq_dev = alphas.shape[1]
    count = 2 * seq_dev
    blocks_here, window, width = left_blocks.shape
    local_k, rows_right, nblocks = right_blocks.shape
    rows_left = window // (2 * CHIPS)
    tokens = emission.shape[0]
    scale = window * nblocks / (2.0 * seq_dev * lax.axis_size("seq"))
    hot = (token_ids.reshape(count, 1) == (jnp.arange(3 * tokens, dtype=jnp.int32) % tokens)[None, :]).astype(BF16)
    part_i, part_k = blocks_here // CHUNKS, local_k // CHUNKS
    rows = nz * blocks_here * local_k
    dma = pltpu.SemaphoreType.DMA
    left_tile = (part_i, rows_left, width)
    right_tile = (part_k, rows_right, nblocks)
    scratch = [
        pltpu.VMEM(alphas.shape, F32),
        pltpu.VMEM(betas.shape, F32),
        pltpu.VMEM(emission.shape, F32),
        pltpu.VMEM(left_blocks.shape, F32),
        pltpu.VMEM((blocks_here, 2 * count, width), BF16),
        pltpu.VMEM((local_k, 2 * count, nblocks), BF16),
        pltpu.VMEM((2 * CHIPS,) + right_blocks.shape, F32),
        pltpu.VMEM((rows, count), F32),
        pltpu.VMEM((rows, count), F32),
        pltpu.VMEM((rows, count), F32),
        pltpu.VMEM((rows, count), F32),
        pltpu.VMEM((CHUNKS, 2, CHIPS) + right_tile, F32),
        pltpu.VMEM((CHUNKS, 2, CHIPS) + left_tile, F32),
        pltpu.VMEM((CHUNKS, CHIPS) + right_tile, F32),
        pltpu.VMEM((CHUNKS, CHIPS) + left_tile, F32),
        pltpu.VMEM((CHIPS - 1, CHUNKS) + right_tile, F32),
        pltpu.VMEM((CHIPS - 1, CHUNKS) + left_tile, F32),
        pltpu.VMEM((8, count), F32),
        pltpu.VMEM((nz - 1, 8, count), F32),
        dma((CHUNKS,)), dma((CHUNKS,)), dma((CHUNKS,)), dma((CHUNKS,)), dma, dma, dma,
        dma((4,)), dma((4,)), dma((3,)), dma((3,)),
        dma((nz - 1,)), dma((nz - 1,)), dma((CHUNKS, nz - 1)), dma((CHUNKS, nz - 1)),
        dma((nz - 1,)), dma((nz - 1,)),
        dma((2 * CHUNKS,)), dma((2 * CHUNKS,)), dma((2 * CHUNKS, 3)), dma((2 * CHUNKS, 3)),
    ]
    anywhere = pl.BlockSpec(memory_space=pl.ANY)
    vmem = pl.BlockSpec(memory_space=pltpu.VMEM)
    return pl.pallas_call(
        functools.partial(kernel, nz, scale),
        out_shape=(
            jax.ShapeDtypeStruct((blocks_here, rows_left, width), F32),
            jax.ShapeDtypeStruct(right_blocks.shape, F32),
        ),
        in_specs=[anywhere, anywhere, vmem, anywhere, anywhere, anywhere],
        out_specs=(vmem, vmem),
        scratch_shapes=scratch,
        compiler_params=pltpu.CompilerParams(
            collective_id=0, has_side_effects=True, vmem_limit_bytes=60 * 2**20
        ),
        cost_estimate=pl.CostEstimate(flops=5 * 10**9, bytes_accessed=20 * 2**20, transcendentals=0),
    )(alphas, betas, hot, emission, left_blocks, right_blocks)


def local(alphas, betas, token_ids, emission, left_blocks, right_blocks):
    if (
        lax.axis_size("seq") == 2 * CHIPS
        and right_blocks.shape[0] % (8 * CHUNKS) == 0
        and right_blocks.shape[1] % 8 == 0
        and left_blocks.shape[0] % CHUNKS == 0
        and left_blocks.shape[1] % (16 * CHIPS) == 0
    ):
        return fused(alphas, betas, token_ids, emission, left_blocks, right_blocks)
    high = lax.Precision.HIGH
    seq_dev = alphas.shape[1]
    count = 2 * seq_dev
    blocks_here, window, width = left_blocks.shape
    local_k, rows_right, nblocks = right_blocks.shape
    scale = window * nblocks / (2.0 * seq_dev * lax.axis_size("seq"))

    right_full = lax.all_gather(right_blocks, "seq", axis=1, tiled=True)
    a_rows = alphas.reshape(count, blocks_here, width)
    mixed = jnp.einsum("ikj,bij->kib", left_blocks, a_rows, precision=high)
    spread = lax.all_to_all(mixed, "blk", split_axis=0, concat_axis=1, tiled=True)
    rows = jnp.take(emission, token_ids.reshape(count), axis=0)
    signal = (rows * betas.reshape(count, -1)).reshape(count, local_k, nblocks)
    back = jnp.einsum("kim,bkm->kib", right_full, signal, precision=high)
    total = lax.psum(jnp.sum(spread * back, axis=(0, 1)), "blk")
    weight = scale / total
    returned = lax.all_to_all(back, "blk", split_axis=1, concat_axis=0, tiled=True)
    right_sum = jnp.einsum("kib,bkm->ikm", spread * weight, signal, precision=high)
    right_rows = lax.psum_scatter(right_sum, "seq", scatter_dimension=0, tiled=True)
    left_sum = jnp.einsum("kib,bij->kij", returned * weight, a_rows, precision=high)
    left_rows = lax.psum_scatter(left_sum, "seq", scatter_dimension=0, tiled=True)
    return (left_rows.transpose(1, 0, 2), right_rows.transpose(1, 0, 2))


def solution(mesh):
    placed = (
        P(None, "seq", "blk"),
        P(None, "seq", "blk"),
        P(None, "seq"),
        P(None, "blk"),
        P("blk", None, None),
        P("blk", "seq", None),
    )
    return jax.shard_map(
        local,
        mesh=mesh,
        in_specs=placed,
        out_specs=(P("blk", "seq", None), P("blk", "seq", None)),
        check_vma=False,
    )
```

profile of v0, /device:TPU:0, one launch (start us, length us, event | category | flops | bytes accessed | tf_op | source)
XLA Modules:
  0.0 102.9 jit_solution(6912133183322899406)
XLA Ops:
  0.6 0.8 eq.17
  1.4 0.7 compare_convert_fusion.hot_ref
  2.1 97.0 %shard_map.77 = (f32[16,16,512]{2,1,0:T(8,128)}, f32[32,8,512]{2,1,0:T(8,128)}) custom-call(f32[2,64,8192]{2,1,0:T(8,128)} %a_hbm.1, f32[2,64,16384]{2,1,0:T(8,128)} %b_hbm.1, bf16[128,96]{1,0:T(8,128)(2,1)} %compare_convert_fusion.hot_ref, f32[32,16384]{1,0:T(8,128)} %e_hbm.1, f32[16,128,512]{2,1,0:T(8,128)} %l_hbm.1, f32[32,8,512]{2,1,0:T(8,128)} %r_hbm.1), custom_call_target="tpu_custom_call" | custom-call | flops 5000000000 | bytes 20971520 | tf_op jit(solution)/shard_map/pallas_call | solution.py:314
  99.1 1.9 %copy.10 = f32[16,16,512]{2,1,0:T(8,128)} copy(f32[16,16,512]{2,1,0:T(8,128)} %get-tuple-element.4) | data formatting | bytes 1048576
  101.0 1.9 %copy.11 = f32[32,8,512]{2,1,0:T(8,128)} copy(f32[32,8,512]{2,1,0:T(8,128)} %get-tuple-element.5) | data formatting | bytes 1048576
  (1 shorter events, 0.0 us)
where the time goes:
time: 103 us
  Pallas kernels  97 us (94%)
  local copies, waits for them, and re-layouts  4.51 us (4%)
    pallas_call x1, Pallas kernels, fused(): pl.pallas_call(functools.partial(kernel, nz, scale), out_shape=(jax.Shape...  97 us
    unnamed x2, local copies, waits for them, and re-layouts  3.75 us

commit v1 on v0

v1 whole, which is shorter than its diff:
```python
import functools
import jax
import jax.numpy as jnp
from jax import lax
from jax.experimental import pallas as pl
from jax.experimental.pallas import tpu as pltpu
from jax.sharding import PartitionSpec as P

F32 = jnp.float32
BF16 = jnp.bfloat16
CHIPS = 4
CHUNKS = 4


def halves(x):
    top = x.astype(BF16)
    rest = (x - top.astype(F32)).astype(BF16)
    return jnp.concatenate([top, rest], axis=0)


def loop(start, extent, body, unroll):
    def step(n, _):
        for v in range(unroll):
            body(start + n * unroll + v)
        return 0

    lax.fori_loop(0, extent // unroll, step, 0)


def nt(a, b):
    return lax.dot_general(a, b, (((1,), (1,)), ((), ())), preferred_element_type=F32)


def kernel(
    nz, scale, a_hbm, b_hbm, ids_ref, e_hbm, l_hbm, r_hbm, left_own, left_got, right_own, right_got,
    a32, b32, e32, l32, a16, g16, rf, us, ur, hs, hr, pr, pl_, rx0r, rx0l, rxar, rxal, rxbr, rxbl, cs, cr,
    load_a, load_l, load_b, load_e, load_r, own_u, own_h, ag_s, ag_r,
    u_s, u_r, h_s, h_r, c_s, c_r, s0_s, s0_r, s1_s, s1_r, s2_s, s2_r, own_g,
):
    seq = lax.axis_index("seq")
    z = lax.axis_index("blk")
    core, chip = seq % 2, seq // 2
    x, y = chip % 2, chip // 2
    sibling = 2 * chip + 1 - core
    across_x = 2 * (2 * y + 1 - x) + core
    across_y = 2 * (2 * (1 - y) + x) + core
    across = 2 * (2 * (1 - y) + 1 - x) + core
    blocks_here, window, width = l32.shape
    local_k, nblocks = g16.shape[0], g16.shape[2]
    count = a16.shape[1] // 2
    inputs = nz * blocks_here
    tokens = e32.shape[0]
    part_i, part_k = blocks_here // CHUNKS, local_k // CHUNKS
    rows_z = blocks_here * local_k
    rows_c = part_i * local_k

    loads_a, loads_l, loads_b, loads_e = [], [], [], []
    for n in range(CHUNKS):
        cols = pl.ds(n * part_i * width, part_i * width)
        loads_a.append(pltpu.make_async_copy(a_hbm.at[:, :, cols], a32.at[:, :, cols], load_a.at[n]))
        some = pl.ds(n * part_i, part_i)
        loads_l.append(pltpu.make_async_copy(l_hbm.at[some], l32.at[some], load_l.at[n]))
        cols = pl.ds(n * part_k * nblocks, part_k * nblocks)
        loads_b.append(pltpu.make_async_copy(b_hbm.at[:, :, cols], b32.at[:, :, cols], load_b.at[n]))
        loads_e.append(pltpu.make_async_copy(e_hbm.at[:, cols], e32.at[:, cols], load_e.at[n]))
    load_own = pltpu.make_async_copy(r_hbm, rf.at[seq], load_r)
    for n in range(CHUNKS):
        loads_l[n].start()
        loads_a[n].start()
    load_own.start()
    for n in range(CHUNKS):
        loads_e[n].start()
        loads_b[n].start()

    barrier = pltpu.get_barrier_semaphore()
    for other in (sibling, across_x, across_y):
        pl.semaphore_signal(barrier, inc=1, device_id={"seq": other}, device_id_type=pl.DeviceIdType.MESH)
    for d in range(1, nz):
        pl.semaphore_signal(barrier, inc=1, device_id={"blk": (z + d) % nz}, device_id_type=pl.DeviceIdType.MESH)
    pl.semaphore_wait(barrier, 3 + nz - 1)

    def to_seq(src, dst, send, recv, other):
        return pltpu.make_async_remote_copy(
            src_ref=src, dst_ref=dst, send_sem=send, recv_sem=recv,
            device_id={"seq": other}, device_id_type=pl.DeviceIdType.MESH,
        )

    def to_blk(src, dst, send, recv, other):
        return pltpu.make_async_remote_copy(
            src_ref=src, dst_ref=dst, send_sem=send, recv_sem=recv,
            device_id={"blk": other}, device_id_type=pl.DeviceIdType.MESH,
        )

    started = []

    def gather(n, kind, owner, other, lo=0, size=part_k, own=False):
        some = pl.ds(n * part_k + lo, size)
        slot = rf.at[owner, some]
        copy = to_seq(r_hbm.at[some] if own else slot, slot, ag_s.at[kind, n], ag_r.at[kind, n], other)
        copy.start()
        started.append(copy)
        return copy

    gx, gy, gs, gd, fx, fy, fd = {}, {}, {}, {}, {}, {}, {}
    for n in range(CHUNKS):
        gx[n] = gather(n, 0, seq, across_x, own=True)
        gy[n] = gather(n, 1, seq, across_y, own=True)
        gs[n] = gather(n, 2, seq, sibling, own=True)

    def near(n):
        half = part_k // 2
        gx[n].wait_recv()
        relay_y = gather(n, 3, across_x, across_y, 0, half)
        fx[n] = gather(n, 5, across_x, sibling)
        gy[n].wait_recv()
        relay_x = gather(n, 4, across_y, across_x, half, half)
        fy[n] = gather(n, 6, across_y, sibling)
        gd[n] = (relay_y, relay_x)

    def far(n):
        for copy in gd[n]:
            copy.wait_recv()
        fd[n] = gather(n, 7, across, sibling)

    def u_block(i):
        cols = pl.ds(pl.multiple_of(i * width, width), width)
        a = halves(jnp.concatenate([a32[0, :, cols], a32[1, :, cols]], axis=0))
        a16[i] = a
        both = nt(halves(l32[i]), a)
        u = both[:window, :count] + both[:window, count:] + both[window:, :count]
        for dz in range(nz):
            us[pl.ds(dz * rows_z + i * local_k, local_k), :] = u[dz * local_k:(dz + 1) * local_k]

    u_sends = []
    for n in range(CHUNKS):
        loads_l[n].wait()
        loads_a[n].wait()
        loop(n * part_i, part_i, u_block, 2)
        for d in range(1, nz):
            other = (z + d) % nz
            copy = to_blk(
                us.at[pl.ds(other * rows_z + n * rows_c, rows_c)],
                ur.at[pl.ds(z * rows_z + n * rows_c, rows_c)],
                u_s.at[n, d - 1], u_r.at[n, d - 1], other,
            )
            copy.start()
            u_sends.append(copy)
    u_own = pltpu.make_async_copy(us.at[pl.ds(z * rows_z, rows_z)], ur.at[pl.ds(z * rows_z, rows_z)], own_u)
    u_own.start()

    token = lax.broadcasted_iota(jnp.int32, (128, count // 2), 0) % tokens
    hot = jnp.concatenate(
        [jnp.where(token == ids_ref[t:t + 1, :], 1.0, 0.0).astype(F32) for t in range(2)], axis=1
    )
    hot = jnp.transpose(hot)[:, :3 * tokens].astype(BF16)

    def g_block(k):
        cols = pl.ds(pl.multiple_of(k * nblocks, nblocks), nblocks)
        e = e32[:, cols]
        e1 = e.astype(BF16)
        rest = e - e1.astype(F32)
        e2 = rest.astype(BF16)
        e3 = (rest - e2.astype(F32)).astype(BF16)
        picked = jnp.dot(hot, jnp.concatenate([e1, e2, e3], axis=0), preferred_element_type=F32)
        b = jnp.concatenate([b32[0, :, cols], b32[1, :, cols]], axis=0)
        g16[k] = halves(picked * b)

    def h_block(k):
        r = halves(jnp.concatenate([rf[s, k] for s in range(2 * CHIPS)], axis=0))
        both = nt(r, g16[k])
        h = both[:inputs, :count] + both[:inputs, count:] + both[inputs:, :count]
        hs[pl.ds(k, inputs, stride=local_k), :] = h

    def h_part(n):
        if n == 0:
            load_own.wait()
        for copies in (gs, fx, fy, fd):
            copies[n].wait_recv()
        loop(n * part_k, part_k, h_block, 4)

    for n in range(CHUNKS):
        loads_e[n].wait()
        loads_b[n].wait()
        loop(n * part_k, part_k, g_block, 4)
        near(n)
        if n >= 1:
            far(n - 1)
        if n >= 2:
            h_part(n - 2)
    far(CHUNKS - 1)
    h_part(CHUNKS - 2)
    h_part(CHUNKS - 1)

    u_own.wait()
    for copy in u_sends:
        copy.wait_recv()
    step = 64

    def c_block(n, acc):
        rows = pl.ds(pl.multiple_of(n * step, step), step)
        return acc + jnp.sum((ur[rows, :] * hs[rows, :]).reshape(step // 8, 8, count), axis=0)

    acc = lax.fori_loop(0, nz * rows_z // step, c_block, jnp.zeros((8, count), F32))
    cs[...] = acc
    c_sends = []
    for d in range(1, nz):
        copy = to_blk(cs, cr.at[d - 1], c_s.at[d - 1], c_r.at[d - 1], (z + d) % nz)
        copy.start()
        c_sends.append(copy)
    h_own = pltpu.make_async_copy(hs.at[pl.ds(z * rows_z, rows_z)], hr.at[pl.ds(z * rows_z, rows_z)], own_h)
    h_own.start()
    h_sends = []
    for n in range(CHUNKS):
        for d in range(1, nz):
            other = (z + d) % nz
            copy = to_blk(
                hs.at[pl.ds(other * rows_z + n * rows_c, rows_c)],
                hr.at[pl.ds(z * rows_z + n * rows_c, rows_c)],
                h_s.at[n, d - 1], h_r.at[n, d - 1], other,
            )
            copy.start()
            h_sends.append(copy)
    total = acc
    for n, copy in enumerate(c_sends):
        copy.wait_recv()
        total = total + cr[n]
    weight = scale / jnp.sum(total, axis=0, keepdims=True)

    def right_part(n):
        def block(kk):
            k = n * part_k + kk
            u = halves(ur[pl.ds(k, inputs, stride=local_k), :] * weight)
            both = jnp.dot(jnp.concatenate([u, u], axis=1), g16[k], preferred_element_type=F32)
            grad = both[:inputs] + both[inputs:]
            rows = inputs // (2 * CHIPS)
            for s in range(2 * CHIPS):
                pr[n, s % 2, s // 4, s // 2 % 2, kk] = grad[s * rows:(s + 1) * rows]

        loop(0, part_k, block, 4)

    def left_part(n):
        def block(ii):
            i = n * part_i + ii
            h = jnp.concatenate(
                [hr[pl.ds(pl.multiple_of(sz * rows_z + i * local_k, local_k), local_k), :] for sz in range(nz)], axis=0
            )
            h = halves(h * weight)
            both = jnp.dot(jnp.concatenate([h, h], axis=1), a16[i], preferred_element_type=F32)
            grad = both[:window] + both[window:]
            rows = window // (2 * CHIPS)
            for s in range(2 * CHIPS):
                pl_[n, s % 2, s // 4, s // 2 % 2, ii] = grad[s * rows:(s + 1) * rows]

        loop(0, part_i, block, 2)

    firsts, seconds, thirds, kept = {}, {}, {}, []

    def first(m):
        mine, rx0 = (pr, rx0r) if m < CHUNKS else (pl_, rx0l)
        n = m % CHUNKS
        firsts[m] = to_seq(mine.at[n, 1 - core], rx0.at[n], s0_s.at[m], s0_r.at[m], sibling)
        firsts[m].start()

    def second(m):
        mine, rx0, rxa, rxb = (pr, rx0r, rxar, rxbr) if m < CHUNKS else (pl_, rx0l, rxal, rxbl)
        n = m % CHUNKS
        half = mine.shape[4] // 2
        firsts[m].wait_recv()
        for p in range(2):
            for q in range(2):
                mine[n, core, p, q] = mine[n, core, p, q] + rx0[n, p, q]
        copy_x = to_seq(
            mine.at[n, core, :, 1 - x, pl.ds(0, half)], rxa.at[n], s1_s.at[m, 0], s1_r.at[m, 0], across_x
        )
        copy_y = to_seq(
            mine.at[n, core, 1 - y, :, pl.ds(half, half)], rxb.at[n], s1_s.at[m, 1], s1_r.at[m, 1], across_y
        )
        copy_x.start()
        copy_y.start()
        seconds[m] = (copy_x, copy_y)

    def third(m):
        mine, rxa, rxb, own, got = (
            (pr, rxar, rxbr, right_own, right_got) if m < CHUNKS else (pl_, rxal, rxbl, left_own, left_got)
        )
        n = m % CHUNKS
        part = mine.shape[4]
        half = part // 2
        low, top = pl.ds(0, half), pl.ds(half, half)
        seconds[m][0].wait_recv()
        mine[n, core, 1 - y, x, low] = mine[n, core, 1 - y, x, low] + rxa[n, 1 - y]
        copy_y = to_seq(
            mine.at[n, core, 1 - y, x, low], got.at[pl.ds(n * part, half)], s2_s.at[m, 0], s2_r.at[m, 0], across_y
        )
        copy_y.start()
        seconds[m][1].wait_recv()
        mine[n, core, y, 1 - x, top] = mine[n, core, y, 1 - x, top] + rxb[n, 1 - x]
        copy_x = to_seq(
            mine.at[n, core, y, 1 - x, top], got.at[pl.ds(n * part + half, half)], s2_s.at[m, 1], s2_r.at[m, 1], across_x
        )
        copy_x.start()
        thirds[m] = (copy_y, copy_x)
        mine[n, core, y, x, low] = mine[n, core, y, x, low] + rxa[n, y]
        mine[n, core, y, x, top] = mine[n, core, y, x, top] + rxb[n, x]
        keep = pltpu.make_async_copy(mine.at[n, core, y, x], own.at[pl.ds(n * part, part)], own_g.at[m])
        keep.start()
        kept.append(keep)

    for m in range(2 * CHUNKS):
        n = m % CHUNKS
        if m < CHUNKS:
            right_part(n)
        else:
            if n == 0:
                h_own.wait()
            for copy in h_sends[n * (nz - 1):(n + 1) * (nz - 1)]:
                copy.wait_recv()
            left_part(n)
        first(m)
        if m >= 1:
            second(m - 1)
        if m >= 2:
            third(m - 2)
    second(2 * CHUNKS - 1)
    third(2 * CHUNKS - 2)
    third(2 * CHUNKS - 1)

    for copies in thirds.values():
        for copy in copies:
            copy.wait()
    for copy in kept:
        copy.wait()
    for copy in started + u_sends + c_sends + h_sends + list(firsts.values()):
        copy.wait_send()
    for copies in seconds.values():
        for copy in copies:
            copy.wait_send()


def fused(alphas, betas, token_ids, emission, left_blocks, right_blocks):
    nz = lax.axis_size("blk")
    seq_dev = alphas.shape[1]
    count = 2 * seq_dev
    blocks_here, window, width = left_blocks.shape
    local_k, rows_right, nblocks = right_blocks.shape
    rows_left = window // (2 * CHIPS)
    scale = window * nblocks / (2.0 * seq_dev * lax.axis_size("seq"))
    part_i, part_k = blocks_here // CHUNKS, local_k // CHUNKS
    rows = nz * blocks_here * local_k
    dma = pltpu.SemaphoreType.DMA
    left_tile = (part_i, rows_left, width)
    right_tile = (part_k, rows_right, nblocks)
    left_half = (part_i // 2, rows_left, width)
    right_half = (part_k // 2, rows_right, nblocks)
    scratch = [
        pltpu.VMEM(alphas.shape, F32),
        pltpu.VMEM(betas.shape, F32),
        pltpu.VMEM(emission.shape, F32),
        pltpu.VMEM(left_blocks.shape, F32),
        pltpu.VMEM((blocks_here, 2 * count, width), BF16),
        pltpu.VMEM((local_k, 2 * count, nblocks), BF16),
        pltpu.VMEM((2 * CHIPS,) + right_blocks.shape, F32),
        pltpu.VMEM((rows, count), F32),
        pltpu.VMEM((rows, count), F32),
        pltpu.VMEM((rows, count), F32),
        pltpu.VMEM((rows, count), F32),
        pltpu.VMEM((CHUNKS, 2, 2, 2) + right_tile, F32),
        pltpu.VMEM((CHUNKS, 2, 2, 2) + left_tile, F32),
        pltpu.VMEM((CHUNKS, 2, 2) + right_tile, F32),
        pltpu.VMEM((CHUNKS, 2, 2) + left_tile, F32),
        pltpu.VMEM((CHUNKS, 2) + right_half, F32),
        pltpu.VMEM((CHUNKS, 2) + left_half, F32),
        pltpu.VMEM((CHUNKS, 2) + right_half, F32),
        pltpu.VMEM((CHUNKS, 2) + left_half, F32),
        pltpu.VMEM((8, count), F32),
        pltpu.VMEM((nz - 1, 8, count), F32),
        dma((CHUNKS,)), dma((CHUNKS,)), dma((CHUNKS,)), dma((CHUNKS,)), dma, dma, dma,
        dma((8, CHUNKS)), dma((8, CHUNKS)),
        dma((CHUNKS, nz - 1)), dma((CHUNKS, nz - 1)), dma((CHUNKS, nz - 1)), dma((CHUNKS, nz - 1)),
        dma((nz - 1,)), dma((nz - 1,)),
        dma((2 * CHUNKS,)), dma((2 * CHUNKS,)), dma((2 * CHUNKS, 2)), dma((2 * CHUNKS, 2)),
        dma((2 * CHUNKS, 2)), dma((2 * CHUNKS, 2)), dma((2 * CHUNKS,)),
    ]
    anywhere = pl.BlockSpec(memory_space=pl.ANY)
    vmem = pl.BlockSpec(memory_space=pltpu.VMEM)
    left_out = jax.ShapeDtypeStruct((blocks_here, rows_left, width), F32)
    right_out = jax.ShapeDtypeStruct(right_blocks.shape, F32)
    left_own, left_got, right_own, right_got = pl.pallas_call(
        functools.partial(kernel, nz, scale),
        out_shape=(left_out, left_out, right_out, right_out),
        in_specs=[anywhere, anywhere, vmem, anywhere, anywhere, anywhere],
        out_specs=(anywhere,) * 4,
        scratch_shapes=scratch,
        compiler_params=pltpu.CompilerParams(
            collective_id=0, has_side_effects=True, vmem_limit_bytes=60 * 2**20
        ),
        cost_estimate=pl.CostEstimate(flops=5 * 10**9, bytes_accessed=20 * 2**20, transcendentals=0),
    )(alphas, betas, token_ids, emission, left_blocks, right_blocks)
    return (left_own + left_got, right_own + right_got)


def local(alphas, betas, token_ids, emission, left_blocks, right_blocks):
    if (
        lax.axis_size("seq") == 2 * CHIPS
        and right_blocks.shape[0] % (8 * CHUNKS) == 0
        and right_blocks.shape[1] % 8 == 0
        and left_blocks.shape[0] % (2 * CHUNKS) == 0
        and 3 * emission.shape[0] <= 128
        and left_blocks.shape[1] % (16 * CHIPS) == 0
    ):
        return fused(alphas, betas, token_ids, emission, left_blocks, right_blocks)
    high = lax.Precision.HIGH
    seq_dev = alphas.shape[1]
    count = 2 * seq_dev
    blocks_here, window, width = left_blocks.shape
    local_k, rows_right, nblocks = right_blocks.shape
    scale = window * nblocks / (2.0 * seq_dev * lax.axis_size("seq"))

    right_full = lax.all_gather(right_blocks, "seq", axis=1, tiled=True)
    a_rows = alphas.reshape(count, blocks_here, width)
    mixed = jnp.einsum("ikj,bij->kib", left_blocks, a_rows, precision=high)
    spread = lax.all_to_all(mixed, "blk", split_axis=0, concat_axis=1, tiled=True)
    rows = jnp.take(emission, token_ids.reshape(count), axis=0)
    signal = (rows * betas.reshape(count, -1)).reshape(count, local_k, nblocks)
    back = jnp.einsum("kim,bkm->kib", right_full, signal, precision=high)
    total = lax.psum(jnp.sum(spread * back, axis=(0, 1)), "blk")
    weight = scale / total
    returned = lax.all_to_all(back, "blk", split_axis=1, concat_axis=0, tiled=True)
    right_sum = jnp.einsum("kib,bkm->ikm", spread * weight, signal, precision=high)
    right_rows = lax.psum_scatter(right_sum, "seq", scatter_dimension=0, tiled=True)
    left_sum = jnp.einsum("kib,bij->kij", returned * weight, a_rows, precision=high)
    left_rows = lax.psum_scatter(left_sum, "seq", scatter_dimension=0, tiled=True)
    return (left_rows.transpose(1, 0, 2), right_rows.transpose(1, 0, 2))


def solution(mesh):
    placed = (
        P(None, "seq", "blk"),
        P(None, "seq", "blk"),
        P(None, "seq"),
        P(None, "blk"),
        P("blk", None, None),
        P("blk", "seq", None),
    )
    return jax.shard_map(
        local,
        mesh=mesh,
        in_specs=placed,
        out_specs=(P("blk", "seq", None), P("blk", "seq", None)),
        check_vma=False,
    )
```

time: 103 us -> 80.9 us (0.79)
  Pallas kernels: 97 us -> 75.9 us
  local copies, waits for them, and re-layouts: 4.51 us -> 0 us
  other arithmetic: 0.7 us -> 4.16 us
    pallas_call x1, Pallas kernels: 97 us -> 75.9 us  [fused(): pl.pallas_call(functools.partial(kernel, nz, scale), out_shape=(left_out,...]
    add x0 -> x2, other arithmetic: none -> 4.16 us  [fused(): return (left_own + left_got, right_own + right_got)]
    unnamed x2 -> x0, local copies, waits for them, and re-layouts: 3.75 us -> none
where the time goes in v1:
time: 80.9 us; the launch traced here: 80.7 us
  Pallas kernels  75.9 us (94%)
  other arithmetic  4.16 us (5%)
    pallas_call x1, Pallas kernels, fused(): pl.pallas_call(functools.partial(kernel, nz, scale), out_shape=(left_out,...  75.9 us
    add x2, other arithmetic, fused(): return (left_own + left_got, right_own + right_got)  4.16 us

profile of v1, /device:TPU:0, one launch (start us, length us, event | category | flops | bytes accessed | tf_op | source)
XLA Modules:
  0.0 80.7 jit_solution(3514473065197329832)
XLA Ops:
  0.6 75.9 %shard_map.77 = (f32[16,16,512]{2,1,0:T(8,128)}, f32[16,16,512]{2,1,0:T(8,128)}, f32[32,8,512]{2,1,0:T(8,128)}, f32[32,8,512]{2,1,0:T(8,128)}) custom-call(f32[2,64,8192]{2,1,0:T(8,128)} %a_hbm.1, f32[2,64,16384]{2,1,0:T(8,128)} %b_hbm.1, s32[2,64]{1,0:T(2,128)} %ids_ref.1, f32[32,16384]{1,0:T(8,128)} %e_hbm.1, f32[16,128,512]{2,1,0:T(8,128)} %l_hbm.1, ...), custom_call_target="tpu_custom_call" | custom-call | flops 5000000000 | bytes 20971520 | tf_op jit(solution)/shard_map/pallas_call | solution.py:388
  76.5 2.1 %add.6 = f32[16,16,512]{2,1,0:T(8,128)} add(f32[16,16,512]{2,1,0:T(8,128)} %get-tuple-element.6, f32[16,16,512]{2,1,0:T(8,128)} %get-tuple-element.7) | non-fusion elementwise | flops 131072 | bytes 1572864 | tf_op jit(solution)/shard_map/add | solution.py:399
  78.6 2.1 %add.7 = f32[32,8,512]{2,1,0:T(8,128)} add(f32[32,8,512]{2,1,0:T(8,128)} %get-tuple-element.8, f32[32,8,512]{2,1,0:T(8,128)} %get-tuple-element.9) | non-fusion elementwise | flops 131072 | bytes 1572864 | tf_op jit(solution)/shard_map/add | solution.py:399

commit v2 on v1

--- a/solution.py
+++ b/solution.py
@@ -9,7 +9,8 @@
 F32 = jnp.float32
 BF16 = jnp.bfloat16
 CHIPS = 4
-CHUNKS = 4
+PARTS = 4
+CHUNKS = 8
 
 
 def halves(x):
@@ -50,12 +51,12 @@
     count = a16.shape[1] // 2
     inputs = nz * blocks_here
     tokens = e32.shape[0]
-    part_i, part_k = blocks_here // CHUNKS, local_k // CHUNKS
+    part_i, part_k = blocks_here // PARTS, local_k // PARTS
     rows_z = blocks_here * local_k
     rows_c = part_i * local_k
 
     loads_a, loads_l, loads_b, loads_e = [], [], [], []
-    for n in range(CHUNKS):
+    for n in range(PARTS):
         cols = pl.ds(n * part_i * width, part_i * width)
         loads_a.append(pltpu.make_async_copy(a_hbm.at[:, :, cols], a32.at[:, :, cols], load_a.at[n]))
         some = pl.ds(n * part_i, part_i)
@@ -64,20 +65,18 @@
         loads_b.append(pltpu.make_async_copy(b_hbm.at[:, :, cols], b32.at[:, :, cols], load_b.at[n]))
         loads_e.append(pltpu.make_async_copy(e_hbm.at[:, cols], e32.at[:, cols], load_e.at[n]))
     load_own = pltpu.make_async_copy(r_hbm, rf.at[seq], load_r)
-    for n in range(CHUNKS):
+    for n in range(PARTS):
         loads_l[n].start()
         loads_a[n].start()
     load_own.start()
-    for n in range(CHUNKS):
-        loads_e[n].start()
-        loads_b[n].start()
+
+    steps = (2, 3 - 2 * (z % 2), 1 + 2 * (z % 2)) if nz == 4 else tuple(range(1, nz))
 
     barrier = pltpu.get_barrier_semaphore()
     for other in (sibling, across_x, across_y):
         pl.semaphore_signal(barrier, inc=1, device_id={"seq": other}, device_id_type=pl.DeviceIdType.MESH)
     for d in range(1, nz):
         pl.semaphore_signal(barrier, inc=1, device_id={"blk": (z + d) % nz}, device_id_type=pl.DeviceIdType.MESH)
-    pl.semaphore_wait(barrier, 3 + nz - 1)
 
     def to_seq(src, dst, send, recv, other):
         return pltpu.make_async_remote_copy(
@@ -93,8 +92,8 @@
 
     started = []
 
-    def gather(n, kind, owner, other, lo=0, size=part_k, own=False):
-        some = pl.ds(n * part_k + lo, size)
+    def gather(n, kind, owner, other, lo=0, size=local_k // PARTS, own=False):
+        some = pl.ds(n * (local_k // PARTS) + lo, size)
         slot = rf.at[owner, some]
         copy = to_seq(r_hbm.at[some] if own else slot, slot, ag_s.at[kind, n], ag_r.at[kind, n], other)
         copy.start()
@@ -102,10 +101,6 @@
         return copy
 
     gx, gy, gs, gd, fx, fy, fd = {}, {}, {}, {}, {}, {}, {}
-    for n in range(CHUNKS):
-        gx[n] = gather(n, 0, seq, across_x, own=True)
-        gy[n] = gather(n, 1, seq, across_y, own=True)
-        gs[n] = gather(n, 2, seq, sibling, own=True)
 
     def near(n):
         half = part_k // 2
@@ -132,19 +127,28 @@
             us[pl.ds(dz * rows_z + i * local_k, local_k), :] = u[dz * local_k:(dz + 1) * local_k]
 
     u_sends = []
-    for n in range(CHUNKS):
+    for n in range(PARTS):
         loads_l[n].wait()
         loads_a[n].wait()
         loop(n * part_i, part_i, u_block, 2)
-        for d in range(1, nz):
+        if n == 0:
+            pl.semaphore_wait(barrier, 3 + nz - 1)
+        for o, d in enumerate(steps):
             other = (z + d) % nz
             copy = to_blk(
                 us.at[pl.ds(other * rows_z + n * rows_c, rows_c)],
                 ur.at[pl.ds(z * rows_z + n * rows_c, rows_c)],
-                u_s.at[n, d - 1], u_r.at[n, d - 1], other,
+                u_s.at[n, o], u_r.at[n, o], other,
             )
             copy.start()
             u_sends.append(copy)
+        if n == 0:
+            for p in range(PARTS):
+                gx[p] = gather(p, 0, seq, across_x, own=True)
+                gy[p] = gather(p, 1, seq, across_y, own=True)
+                gs[p] = gather(p, 2, seq, sibling, own=True)
+        loads_e[n].start()
+        loads_b[n].start()
     u_own = pltpu.make_async_copy(us.at[pl.ds(z * rows_z, rows_z)], ur.at[pl.ds(z * rows_z, rows_z)], own_u)
     u_own.start()
 
@@ -178,7 +182,7 @@
             copies[n].wait_recv()
         loop(n * part_k, part_k, h_block, 4)
 
-    for n in range(CHUNKS):
+    for n in range(PARTS):
         loads_e[n].wait()
         loads_b[n].wait()
         loop(n * part_k, part_k, g_block, 4)
@@ -187,20 +191,20 @@
             far(n - 1)
         if n >= 2:
             h_part(n - 2)
-    far(CHUNKS - 1)
-    h_part(CHUNKS - 2)
-    h_part(CHUNKS - 1)
-
+    far(PARTS - 1)
+    h_part(PARTS - 2)
+    h_part(PARTS - 1)
+
+    step = 64
+    acc = jnp.zeros((8, count), F32)
     u_own.wait()
-    for copy in u_sends:
-        copy.wait_recv()
-    step = 64
-
-    def c_block(n, acc):
-        rows = pl.ds(pl.multiple_of(n * step, step), step)
-        return acc + jnp.sum((ur[rows, :] * hs[rows, :]).reshape(step // 8, 8, count), axis=0)
-
-    acc = lax.fori_loop(0, nz * rows_z // step, c_block, jnp.zeros((8, count), F32))
+    for n in range(PARTS):
+        for copy in u_sends[n * (nz - 1):(n + 1) * (nz - 1)]:
+            copy.wait_recv()
+        for sz in range(nz):
+            for lo in range(0, rows_c, step):
+                rows = pl.ds(sz * rows_z + n * rows_c + lo, step)
+                acc = acc + jnp.sum((ur[rows, :] * hs[rows, :]).reshape(step // 8, 8, count), axis=0)
     cs[...] = acc
     c_sends = []
     for d in range(1, nz):
@@ -209,14 +213,16 @@
         c_sends.append(copy)
     h_own = pltpu.make_async_copy(hs.at[pl.ds(z * rows_z, rows_z)], hr.at[pl.ds(z * rows_z, rows_z)], own_h)
     h_own.start()
+    part_i, part_k = blocks_here // CHUNKS, local_k // CHUNKS
+    rows_c = part_i * local_k
     h_sends = []
     for n in range(CHUNKS):
-        for d in range(1, nz):
+        for o, d in enumerate(steps):
             other = (z + d) % nz
             copy = to_blk(
                 hs.at[pl.ds(other * rows_z + n * rows_c, rows_c)],
                 hr.at[pl.ds(z * rows_z + n * rows_c, rows_c)],
-                h_s.at[n, d - 1], h_r.at[n, d - 1], other,
+                h_s.at[n, o], h_r.at[n, o], other,
             )
             copy.start()
             h_sends.append(copy)
@@ -310,17 +316,18 @@
         n = m % CHUNKS
         if m < CHUNKS:
             right_part(n)
-        else:
+            first(m)
+        if m >= 1:
+            second(m - 1)
+        if m >= 2:
+            third(m - 2)
+        if m >= CHUNKS:
             if n == 0:
                 h_own.wait()
             for copy in h_sends[n * (nz - 1):(n + 1) * (nz - 1)]:
                 copy.wait_recv()
             left_part(n)
-        first(m)
-        if m >= 1:
-            second(m - 1)
-        if m >= 2:
-            third(m - 2)
+            first(m)
     second(2 * CHUNKS - 1)
     third(2 * CHUNKS - 2)
     third(2 * CHUNKS - 1)
@@ -335,6 +342,11 @@
     for copies in seconds.values():
         for copy in copies:
             copy.wait_send()
+
+
+def last_sum(left_own, left_got, right_own, right_got, left, right):
+    left[...] = left_own[...] + left_got[...]
+    right[...] = right_own[...] + right_got[...]
 
 
 def fused(alphas, betas, token_ids, emission, left_blocks, right_blocks):
@@ -374,9 +386,9 @@
         pltpu.VMEM((CHUNKS, 2) + left_half, F32),
         pltpu.VMEM((8, count), F32),
         pltpu.VMEM((nz - 1, 8, count), F32),
-        dma((CHUNKS,)), dma((CHUNKS,)), dma((CHUNKS,)), dma((CHUNKS,)), dma, dma, dma,
-        dma((8, CHUNKS)), dma((8, CHUNKS)),
-        dma((CHUNKS, nz - 1)), dma((CHUNKS, nz - 1)), dma((CHUNKS, nz - 1)), dma((CHUNKS, nz - 1)),
+        dma((PARTS,)), dma((PARTS,)), dma((PARTS,)), dma((PARTS,)), dma, dma, dma,
+        dma((8, PARTS)), dma((8, PARTS)),
+        dma((PARTS, nz - 1)), dma((PARTS, nz - 1)), dma((CHUNKS, nz - 1)), dma((CHUNKS, nz - 1)),
         dma((nz - 1,)), dma((nz - 1,)),
         dma((2 * CHUNKS,)), dma((2 * CHUNKS,)), dma((2 * CHUNKS, 2)), dma((2 * CHUNKS, 2)),
         dma((2 * CHUNKS, 2)), dma((2 * CHUNKS, 2)), dma((2 * CHUNKS,)),
@@ -396,13 +408,32 @@
         ),
         cost_estimate=pl.CostEstimate(flops=5 * 10**9, bytes_accessed=20 * 2**20, transcendentals=0),
     )(alphas, betas, token_ids, emission, left_blocks, right_blocks)
-    return (left_own + left_got, right_own + right_got)
+    flat = (-1, width)
+    grid = 4
+    left, right = pl.pallas_call(
+        last_sum,
+        grid=(grid,),
+        out_shape=(
+            jax.ShapeDtypeStruct((left_own.size // width, width), F32),
+            jax.ShapeDtypeStruct((right_own.size // width, width), F32),
+        ),
+        in_specs=[
+            pl.BlockSpec((part.size // width // grid, width), lambda n: (n, 0))
+            for part in (left_own, left_got, right_own, right_got)
+        ],
+        out_specs=tuple(
+            pl.BlockSpec((part.size // width // grid, width), lambda n: (n, 0)) for part in (left_own, right_own)
+        ),
+        compiler_params=pltpu.CompilerParams(vmem_limit_bytes=60 * 2**20),
+    )(left_own.reshape(flat), left_got.reshape(flat), right_own.reshape(flat), right_got.reshape(flat))
+    return left.reshape(left_own.shape), right.reshape(right_own.shape)
 
 
 def local(alphas, betas, token_ids, emission, left_blocks, right_blocks):
     if (
         lax.axis_size("seq") == 2 * CHIPS
-        and right_blocks.shape[0] % (8 * CHUNKS) == 0
+        and right_blocks.shape[0] % (4 * CHUNKS) == 0
+        and right_blocks.shape[2] == left_blocks.shape[2]
         and right_blocks.shape[1] % 8 == 0
         and left_blocks.shape[0] % (2 * CHUNKS) == 0
         and 3 * emission.shape[0] <= 128

time: 80.9 us -> 85.4 us (1.056)
  Pallas kernels: 75.9 us -> 84.6 us
  other arithmetic: 4.16 us -> 0 us
    pallas_call x1, Pallas kernels: 75.9 us -> 81 us  [fused(): pl.pallas_call(functools.partial(kernel, nz, scale), out_shape=(left_out,...]
    add x2 -> x0, other arithmetic: 4.16 us -> none  [fused(): return (left_own + left_got, right_own + right_got)]
    pallas_call x0 -> x1, Pallas kernels: none -> 3.62 us  [fused(): pl.pallas_call(last_sum, grid=(grid,), out_shape=(jax.ShapeDtypeStruct((l...]
where the time goes in v2:
time: 85.4 us; the launch traced here: 85.2 us
  Pallas kernels  84.6 us (99%)
    pallas_call x1, Pallas kernels, fused(): pl.pallas_call(functools.partial(kernel, nz, scale), out_shape=(left_out,...  81 us
    pallas_call x1, Pallas kernels, fused(): pl.pallas_call(last_sum, grid=(grid,), out_shape=(jax.ShapeDtypeStruct((l...  3.62 us

profile of v2, /device:TPU:0, one launch (start us, length us, event | category | flops | bytes accessed | tf_op | source)
XLA Modules:
  0.0 85.2 jit_solution(5361547667041922370)
XLA Ops:
  0.6 81.0 %shard_map.77 = (f32[16,16,512]{2,1,0:T(8,128)}, f32[16,16,512]{2,1,0:T(8,128)}, f32[32,8,512]{2,1,0:T(8,128)}, f32[32,8,512]{2,1,0:T(8,128)}) custom-call(f32[2,64,8192]{2,1,0:T(8,128)} %a_hbm.1, f32[2,64,16384]{2,1,0:T(8,128)} %b_hbm.1, s32[2,64]{1,0:T(2,128)} %ids_ref.1, f32[32,16384]{1,0:T(8,128)} %e_hbm.1, f32[16,128,512]{2,1,0:T(8,128)} %l_hbm.1, ...), custom_call_target="tpu_custom_call" | custom-call | flops 5000000000 | bytes 20971520 | tf_op jit(solution)/shard_map/pallas_call | solution.py:400
  81.6 3.6 %shard_map.78 = (f32[256,512]{1,0:T(8,128)}, f32[256,512]{1,0:T(8,128)}) custom-call(f32[256,512]{1,0:T(8,128)} %bitcast.6, f32[256,512]{1,0:T(8,128)} %bitcast.7, f32[256,512]{1,0:T(8,128)} %bitcast.8, f32[256,512]{1,0:T(8,128)} %bitcast.9), custom_call_target="tpu_custom_call" | custom-call | tf_op jit(solution)/shard_map/pallas_call | solution.py:413

commit v3 on v2

--- a/solution.py
+++ b/solution.py
@@ -312,25 +312,23 @@
         keep.start()
         kept.append(keep)
 
-    for m in range(2 * CHUNKS):
+    last = 2 * CHUNKS
+    for m in range(last + 3):
         n = m % CHUNKS
         if m < CHUNKS:
             right_part(n)
-            first(m)
-        if m >= 1:
-            second(m - 1)
-        if m >= 2:
-            third(m - 2)
-        if m >= CHUNKS:
+        elif m < last:
             if n == 0:
                 h_own.wait()
             for copy in h_sends[n * (nz - 1):(n + 1) * (nz - 1)]:
                 copy.wait_recv()
             left_part(n)
+        if m < last:
             first(m)
-    second(2 * CHUNKS - 1)
-    third(2 * CHUNKS - 2)
-    third(2 * CHUNKS - 1)
+        if 1 <= m <= last:
+            second(m - 1)
+        if m >= 3:
+            third(m - 3)
 
     for copies in thirds.values():
         for copy in copies:
@@ -409,7 +407,7 @@
         cost_estimate=pl.CostEstimate(flops=5 * 10**9, bytes_accessed=20 * 2**20, transcendentals=0),
     )(alphas, betas, token_ids, emission, left_blocks, right_blocks)
     flat = (-1, width)
-    grid = 4
+    grid = 1
     left, right = pl.pallas_call(
         last_sum,
         grid=(grid,),

time: 85.4 us -> 79.1 us (0.926)
  Pallas kernels: 84.6 us -> 78.3 us
    pallas_call x1, Pallas kernels: 81 us -> 75.8 us  [fused(): pl.pallas_call(functools.partial(kernel, nz, scale), out_shape=(left_out,...]
    pallas_call x1, Pallas kernels: 3.62 us -> 2.54 us  [fused(): pl.pallas_call(last_sum, grid=(grid,), out_shape=(jax.ShapeDtypeStruct((l...]
where the time goes in v3:
time: 79.1 us; the launch traced here: 78.9 us
  Pallas kernels  78.3 us (99%)
    pallas_call x1, Pallas kernels, fused(): pl.pallas_call(functools.partial(kernel, nz, scale), out_shape=(left_out,...  75.8 us
    pallas_call x1, Pallas kernels, fused(): pl.pallas_call(last_sum, grid=(grid,), out_shape=(jax.ShapeDtypeStruct((l...  2.54 us

profile of v3, /device:TPU:0, one launch (start us, length us, event | category | flops | bytes accessed | tf_op | source)
XLA Modules:
  0.0 78.9 jit_solution(16521827805216908182)
XLA Ops:
  0.6 75.8 %shard_map.77 = (f32[16,16,512]{2,1,0:T(8,128)}, f32[16,16,512]{2,1,0:T(8,128)}, f32[32,8,512]{2,1,0:T(8,128)}, f32[32,8,512]{2,1,0:T(8,128)}) custom-call(f32[2,64,8192]{2,1,0:T(8,128)} %a_hbm.1, f32[2,64,16384]{2,1,0:T(8,128)} %b_hbm.1, s32[2,64]{1,0:T(2,128)} %ids_ref.1, f32[32,16384]{1,0:T(8,128)} %e_hbm.1, f32[16,128,512]{2,1,0:T(8,128)} %l_hbm.1, ...), custom_call_target="tpu_custom_call" | custom-call | flops 5000000000 | bytes 20971520 | tf_op jit(solution)/shard_map/pallas_call | solution.py:398
  76.4 2.5 %shard_map.78 = (f32[256,512]{1,0:T(8,128)}, f32[256,512]{1,0:T(8,128)}) custom-call(f32[256,512]{1,0:T(8,128)} %bitcast.6, f32[256,512]{1,0:T(8,128)} %bitcast.7, f32[256,512]{1,0:T(8,128)} %bitcast.8, f32[256,512]{1,0:T(8,128)} %bitcast.9), custom_call_target="tpu_custom_call" | custom-call | tf_op jit(solution)/shard_map/pallas_call | solution.py:411

commit v4 on v3

--- a/solution.py
+++ b/solution.py
@@ -69,6 +69,9 @@
         loads_l[n].start()
         loads_a[n].start()
     load_own.start()
+    for n in range(PARTS):
+        loads_e[n].start()
+        loads_b[n].start()
 
     steps = (2, 3 - 2 * (z % 2), 1 + 2 * (z % 2)) if nz == 4 else tuple(range(1, nz))
 
@@ -77,6 +80,8 @@
         pl.semaphore_signal(barrier, inc=1, device_id={"seq": other}, device_id_type=pl.DeviceIdType.MESH)
     for d in range(1, nz):
         pl.semaphore_signal(barrier, inc=1, device_id={"blk": (z + d) % nz}, device_id_type=pl.DeviceIdType.MESH)
+
+    pl.semaphore_wait(barrier, 3 + nz - 1)
 
     def to_seq(src, dst, send, recv, other):
         return pltpu.make_async_remote_copy(
@@ -101,6 +106,10 @@
         return copy
 
     gx, gy, gs, gd, fx, fy, fd = {}, {}, {}, {}, {}, {}, {}
+    for n in range(PARTS):
+        gx[n] = gather(n, 0, seq, across_x, own=True)
+        gy[n] = gather(n, 1, seq, across_y, own=True)
+        gs[n] = gather(n, 2, seq, sibling, own=True)
 
     def near(n):
         half = part_k // 2
@@ -131,8 +140,6 @@
         loads_l[n].wait()
         loads_a[n].wait()
         loop(n * part_i, part_i, u_block, 2)
-        if n == 0:
-            pl.semaphore_wait(barrier, 3 + nz - 1)
         for o, d in enumerate(steps):
             other = (z + d) % nz
             copy = to_blk(
@@ -142,13 +149,6 @@
             )
             copy.start()
             u_sends.append(copy)
-        if n == 0:
-            for p in range(PARTS):
-                gx[p] = gather(p, 0, seq, across_x, own=True)
-                gy[p] = gather(p, 1, seq, across_y, own=True)
-                gs[p] = gather(p, 2, seq, sibling, own=True)
-        loads_e[n].start()
-        loads_b[n].start()
     u_own = pltpu.make_async_copy(us.at[pl.ds(z * rows_z, rows_z)], ur.at[pl.ds(z * rows_z, rows_z)], own_u)
     u_own.start()
 

time: 79.1 us -> 79 us (level)
  no operation moved by 1% of the time
where the time goes in v4:
time: 79 us; the launch traced here: 78.8 us
  Pallas kernels  78.2 us (99%)
    pallas_call x1, Pallas kernels, fused(): pl.pallas_call(functools.partial(kernel, nz, scale), out_shape=(left_out,...  75.7 us
    pallas_call x1, Pallas kernels, fused(): pl.pallas_call(last_sum, grid=(grid,), out_shape=(jax.ShapeDtypeStruct((l...  2.54 us

profile of v4, /device:TPU:0, one launch (start us, length us, event | category | flops | bytes accessed | tf_op | source)
XLA Modules:
  0.0 78.8 jit_solution(12826171795059716447)
XLA Ops:
  0.6 75.7 %shard_map.77 = (f32[16,16,512]{2,1,0:T(8,128)}, f32[16,16,512]{2,1,0:T(8,128)}, f32[32,8,512]{2,1,0:T(8,128)}, f32[32,8,512]{2,1,0:T(8,128)}) custom-call(f32[2,64,8192]{2,1,0:T(8,128)} %a_hbm.1, f32[2,64,16384]{2,1,0:T(8,128)} %b_hbm.1, s32[2,64]{1,0:T(2,128)} %ids_ref.1, f32[32,16384]{1,0:T(8,128)} %e_hbm.1, f32[16,128,512]{2,1,0:T(8,128)} %l_hbm.1, ...), custom_call_target="tpu_custom_call" | custom-call | flops 5000000000 | bytes 20971520 | tf_op jit(solution)/shard_map/pallas_call | solution.py:398
  76.3 2.5 %shard_map.78 = (f32[256,512]{1,0:T(8,128)}, f32[256,512]{1,0:T(8,128)}) custom-call(f32[256,512]{1,0:T(8,128)} %bitcast.6, f32[256,512]{1,0:T(8,128)} %bitcast.7, f32[256,512]{1,0:T(8,128)} %bitcast.8, f32[256,512]{1,0:T(8,128)} %bitcast.9), custom_call_target="tpu_custom_call" | custom-call | tf_op jit(solution)/shard_map/pallas_call | solution.py:411
